TPU v7x, 512 devices: a whole 4x8x8 slice. The times are simulated.
512 devices in a mesh: ha: 8 (over y), wa: 16 (over z, x_hi), fsdp: 4 (over x_lo, core).
Axes of the slice: x: 4 (x_hi: 2, x_lo: 2; x = x_hi * 2 + x_lo), y: 8, z: 8, core: 2. Of those that a mesh axis runs over, the one named last changes fastest.
Arguments:
- latent: bfloat16 [4, 1, 128, 128, 1536], P('fsdp', None, 'ha', 'wa'), may hold values from -6 to 6
- qkv_weight: bfloat16 [1536, 12, 384], P(None, 'fsdp'), may hold values from -0.15625 to 0.15625
- query_gain: float32 [128], replicated, may hold values from 0.1 to 1.9
- key_gain: float32 [128], replicated, may hold values from 0.1 to 1.9
Outputs:
- attended: bfloat16 [4, 1, 128, 128, 1536], P('fsdp', None, 'ha', 'wa')
All inputs are finite; a program needn't handle non-finite values.
Results may differ from a plain program's by a relative error of at most 0.011.
Values may be sent and summed in bfloat16 or wider, within the bound.
A program may use at most 64 MiB of HBM per device.

v0:
```python
import math

import jax
import jax.numpy as jnp
import numpy as np
from jax import lax
from jax.sharding import PartitionSpec as P

WIN = 8


def padded_2(cells, sides, width):
    for axis, dim in sides:
        count = lax.axis_size(axis)
        head = lax.slice_in_dim(cells, 0, width, axis=dim)
        tail = lax.slice_in_dim(cells, cells.shape[dim] - width, cells.shape[dim], axis=dim)
        cells = jnp.concatenate(
            [
                lax.ppermute(tail, axis, [(i, (i + 1) % count) for i in range(count)]),
                cells,
                lax.ppermute(head, axis, [((i + 1) % count, i) for i in range(count)]),
            ],
            axis=dim,
        )
    return cells


def rms_gain(part, gain):
    values32 = part.astype(jnp.float32)
    scale = lax.rsqrt(jnp.mean(values32 * values32, axis=-1, keepdims=True) + 1e-06)
    return (values32 * scale * gain).astype(jnp.bfloat16)


def attend(packed, query_gain, key_gain):
    batch_count, frame_count, row_count, col_count, head_count, triple_width = packed.shape
    head_dim = triple_width // 3
    half_win = WIN // 2
    queries = rms_gain(packed[..., :head_dim], query_gain)
    keyed = rms_gain(packed[..., head_dim : 2 * head_dim], key_gain)
    joined = jnp.concatenate([keyed, packed[..., 2 * head_dim :]], axis=-1)
    padded = padded_2(joined, (("ha", 2), ("wa", 3)), half_win)
    row_windows = row_count // WIN + 1
    col_windows = col_count // WIN + 1
    windowed = padded.reshape(
        batch_count, frame_count, row_windows, WIN, col_windows, WIN, head_count, 2 * head_dim
    )
    tile_rows = row_count // half_win
    tile_cols = col_count // half_win
    row_pick = np.array([(index + 1) // 2 for index in range(tile_rows)], dtype=np.int32)
    col_pick = np.array([(index + 1) // 2 for index in range(tile_cols)], dtype=np.int32)
    chosen = jnp.take(windowed, row_pick, axis=2)
    chosen = jnp.take(chosen, col_pick, axis=4)
    context = chosen.transpose(0, 2, 4, 6, 1, 3, 5, 7).reshape(
        batch_count, tile_rows, tile_cols, head_count, frame_count * WIN * WIN, 2 * head_dim
    )
    grouped = queries.reshape(
        batch_count, frame_count, tile_rows, half_win, tile_cols, half_win, head_count, head_dim
    )
    grouped = grouped.transpose(0, 2, 4, 6, 1, 3, 5, 7).reshape(
        batch_count, tile_rows, tile_cols, head_count, frame_count * half_win * half_win, head_dim
    )
    scores = jnp.einsum(
        "nabhqe,nabhke->nabhqk",
        grouped,
        context[..., :head_dim],
        preferred_element_type=jnp.float32,
    ) / math.sqrt(head_dim)
    probs = jax.nn.softmax(scores, axis=-1).astype(jnp.bfloat16)
    blended = jnp.einsum(
        "nabhqk,nabhke->nabhqe", probs, context[..., head_dim:], preferred_element_type=jnp.float32
    ).astype(jnp.bfloat16)
    blended = blended.reshape(
        batch_count, tile_rows, tile_cols, head_count, frame_count, half_win, half_win, head_dim
    )
    blended = blended.transpose(0, 4, 1, 5, 2, 6, 3, 7)
    return blended.reshape(batch_count, frame_count, row_count, col_count, head_count * head_dim)


def shards(latent, qkv_weight, query_gain, key_gain):
    token_rows = latent.reshape(-1, latent.shape[-1])
    packed = jnp.einsum(
        "td,dge->tge",
        token_rows,
        lax.all_gather(qkv_weight, "fsdp", axis=1, tiled=True),
        preferred_element_type=jnp.float32,
    ).astype(jnp.bfloat16)
    packed = packed.reshape(latent.shape[:4] + packed.shape[1:])
    return attend(packed, query_gain, key_gain)


def solution(mesh):
    return jax.shard_map(
        shards,
        mesh=mesh,
        in_specs=(P("fsdp", None, "ha", "wa", None), P(None, "fsdp", None), P(), P()),
        out_specs=P("fsdp", None, "ha", "wa", None),
        check_vma=False,
    )
```

profile of v0, /device:TPU:25, one launch (start us, length us, event | category | flops | bytes accessed | tf_op | source)
XLA Modules:
  0.0 237.5 jit_solution(13623455065030111685)
XLA Ops:
  6.5 0.7 all-gather.2.cloned.1.call-update
  7.3 141.7 %all-gather.2.cloned.1.call-done = bf16[1536,12,384]{2,0,1:T(8,128)(2,1)} async-done(((bf16[1536,3,384]{2,0,1:T(8,128)(2,1)}), bf16[1536,12,384]{2,0,1:T(8,128)(2,1)}) %all-gather.2.cloned.1.call-update) | async-done | bytes 14155792 | tf_op jit(solution)/shard_map/all_gather | solution.py:84
  149.0 7.0 %fusion.4 = bf16[1,1,16,8,12,384]{5,3,2,4,1,0:T(8,128)(2,1)S(1)} fusion(bf16[1536,12,384]{2,0,1:T(8,128)(2,1)} %all-gather.2.cloned.1.call-done, bf16[1,1,16,8,1536]{4,3,2,1,0:T(8,128)(2,1)S(1)} %copy-done), kind=kOutput, calls=%fused_computation.15 | convolution fusion | flops 1812529152 | bytes 15728640 | tf_op jit(solution)/shard_map/td,dge->tge/dot_general | solution.py:81
  156.0 0.2 fusion.19
  156.3 0.3 fusion.12
  156.8 0.3 fusion.14
  157.1 4.3 %collective-permute-start = (bf16[1,1,4,8,12,256]{5,3,4,2,1,0:T(8,128)(2,1)S(1)}, bf16[1,1,4,8,12,256]{5,3,4,2,1,0:T(8,128)(2,1)S(1)}, u32[]{:S(2)}, u32[]{:S(2)}) collective-permute-start(bf16[1,1,4,8,12,256]{5,3,4,2,1,0:T(8,128)(2,1)S(1)} %get-tuple-element.11), channel_id=1, source_target_pairs={{0,64},{64,128},{128,192},{192,256},{256,320},{320,384},{384,448},... | collective-permute-start | bytes 589832 | tf_op jit(solution)/shard_map/ppermute | solution.py:19
  161.5 1.9 collective-permute-start.1
  163.4 1.7 collective-permute-done
  165.2 5.3 %collective-permute-done.1 = bf16[1,1,4,8,12,256]{5,3,4,2,1,0:T(8,128)(2,1)S(1)} collective-permute-done((bf16[1,1,4,8,12,256]{5,3,4,2,1,0:T(8,128)(2,1)S(1)}, bf16[1,1,4,8,12,256]{5,3,4,2,1,0:T(8,128)(2,1)S(1)}, u32[]{:S(2)}, u32[]{:S(2)}) %collective-permute-start.1) | collective-permute-done | bytes 196640 | tf_op jit(solution)/shard_map/ppermute | solution.py:21
  170.5 0.1 pad_maximum_fusion.1
  170.6 1.4 fusion.18
  172.0 4.6 %collective-permute-start.2 = (bf16[1,1,24,4,12,256]{5,3,4,2,1,0:T(4,128)(2,1)}, bf16[1,1,24,4,12,256]{5,3,4,2,1,0:T(4,128)(2,1)S(1)}, u32[]{:S(2)}, u32[]{:S(2)}) collective-permute-start(bf16[1,1,24,4,12,256]{5,3,4,2,1,0:T(4,128)(2,1)} %get-tuple-element.7), channel_id=1, source_target_pairs={{0,4},{4,8},{8,12},{12,16},{16,20},{20,24},{24,28},{28,32},{32,36}... | collective-permute-start | bytes 1769480 | tf_op jit(solution)/shard_map/ppermute | solution.py:19
  176.6 5.3 %collective-permute-start.3 = (bf16[1,1,24,4,12,256]{5,3,4,2,1,0:T(4,128)(2,1)}, bf16[1,1,24,4,12,256]{5,3,4,2,1,0:T(4,128)(2,1)}, u32[]{:S(2)}, u32[]{:S(2)}) collective-permute-start(bf16[1,1,24,4,12,256]{5,3,4,2,1,0:T(4,128)(2,1)} %get-tuple-element.8), channel_id=1, source_target_pairs={{4,0},{8,4},{12,8},{16,12},{20,16},{24,20},{28,24},{32,28},{36,32}... | collective-permute-start | bytes 1769480 | tf_op jit(solution)/shard_map/ppermute | solution.py:21
  181.9 0.3 fusion.9
  182.4 0.3 fusion.11
  182.7 0.9 copy.39
  183.6 18.3 %collective-permute-done.2 = bf16[1,1,24,4,12,256]{5,3,4,2,1,0:T(4,128)(2,1)S(1)} collective-permute-done((bf16[1,1,24,4,12,256]{5,3,4,2,1,0:T(4,128)(2,1)}, bf16[1,1,24,4,12,256]{5,3,4,2,1,0:T(4,128)(2,1)S(1)}, u32[]{:S(2)}, u32[]{:S(2)}) %collective-permute-start.2) | collective-permute-done | bytes 589856 | tf_op jit(solution)/shard_map/ppermute | solution.py:19
  201.9 4.8 %collective-permute-done.3 = bf16[1,1,24,4,12,256]{5,3,4,2,1,0:T(4,128)(2,1)} collective-permute-done((bf16[1,1,24,4,12,256]{5,3,4,2,1,0:T(4,128)(2,1)}, bf16[1,1,24,4,12,256]{5,3,4,2,1,0:T(4,128)(2,1)}, u32[]{:S(2)}, u32[]{:S(2)}) %collective-permute-start.3) | collective-permute-done | bytes 589856 | tf_op jit(solution)/shard_map/ppermute | solution.py:21
  206.7 2.9 %pad_maximum_fusion = bf16[1,1,24,16,12,256]{5,3,4,2,1,0:T(8,128)(2,1)S(1)} fusion(bf16[1,1,24,4,12,256]{5,3,4,2,1,0:T(4,128)(2,1)} %collective-permute-done.3, bf16[1,1,4,8,12,256]{5,3,4,2,1,0:T(8,128)(2,1)S(1)} %collective-permute-done.1, bf16[1,1,16,8,12,128]{5,3,4,2,1,0:T(8,128)(2,1)S(1)} %fusion.14, ...), kind=kLoop, calls=%fused_computation.7 | loop fusion | flops 14155776 | bytes 4718592 | tf_op jit(solution)/shard_map/concatenate | solution.py:17
  209.6 0.3 copy.44
  209.9 2.4 %gather_fusion = bf16[4,8,2,8,12,256]{5,3,4,2,1,0:T(8,128)(2,1)} fusion(bf16[3,8,2,8,12,256]{5,3,4,2,1,0:T(8,128)(2,1)S(1)} %copy.44, s32[1024]{0:T(1024)S(1)} %pad_clamp_fusion.1), kind=kCustom, calls=%fused_computation | custom fusion | bytes 6291472 | tf_op jit(solution)/shard_map/jit(_take)/gather | solution.py:51
  212.3 3.3 %slice_bitcast_fusion.5 = (bf16[4,8,2,8,12,128]{5,3,4,2,1,0:T(8,128)(2,1)}, bf16[4,8,2,8,12,128]{5,3,4,2,1,0:T(8,128)(2,1)S(1)}) fusion(bf16[1,1,4,8,2,8,12,256]{7,5,6,4,3,2,1,0:T(8,128)(2,1)} %bitcast.46), kind=kLoop, calls=%fused_computation.13 | loop fusion | bytes 6291456 | tf_op jit(solution)/shard_map/jit(_take)/gather | solution.py:52
  215.6 2.3 gather_fusion.1
  217.9 1.9 gather_fusion.2
  219.8 2.4 %copy_bitcast_fusion = bf16[1,4,2,12,64,256]{5,4,3,2,1,0:T(8,128)(2,1)S(1)} fusion(bf16[1,1,4,8,2,8,12,128]{7,5,6,3,2,4,1,0:T(8,128)(2,1)} %bitcast.49, bf16[1,1,4,8,2,8,12,128]{7,5,6,3,2,4,1,0:T(8,128)(2,1)S(1)} %bitcast.48, pred[2]{0:T(512)(128)(4,1)S(1)} %iota_compare_fusion), kind=kLoop, calls=%fused_computation.6 | loop fusion | flops 7864320 | bytes 6291458 | tf_op jit(solution)/shard_map/reshape | solution.py:53
  222.2 1.6 copy-done.1
  223.9 0.9 fusion.7
  224.8 0.5 fusion.20
  225.3 4.2 %fusion.8 = bf16[4,2,12,16,128]{4,3,2,1,0:T(8,128)(2,1)S(1)} fusion(bf16[1,4,2,12,64,256]{5,4,3,2,1,0:T(8,128)(2,1)} %copy-done.1, f32[4,2,12,16]{3,2,1,0:T(8,128)S(1)} %fusion.20, f32[4,2,12,16,64]{4,3,2,1,0:T(8,128)S(1)} %fusion.7), kind=kOutput, calls=%fused_computation.19 | convolution fusion | flops 25658944 | bytes 3604480 | tf_op jit(solution)/shard_map/nabhqk,nabhke->nabhqe/dot_general | solution.py:69
  229.5 0.1 copy.59
  229.6 1.0 reshape.120
  (23 shorter events, 0.5 us)
Async XLA Ops:
  6.5 142.4 %copy-start = (bf16[1,1,16,8,1536]{4,3,2,1,0:T(8,128)(2,1)S(1)}, bf16[1,1,16,8,1536]{4,3,2,1,0:T(8,128)(2,1)}, u32[]{:S(2)}) copy-start(bf16[1,1,16,8,1536]{4,3,2,1,0:T(8,128)(2,1)} %param.6) | copy-start | bytes 1179652
  6.5 142.4 %all-gather.2.cloned.1.call-start = ((), (), s32[]{:S(2)}) async-start(), calls=%async_computation | async-start | bytes 17694720 | tf_op jit(solution)/shard_map/all_gather | solution.py:84
  156.0 0.8 copy-start.3
  156.0 7.4 %copy-start.5 = (s32[4]{0:T(128)S(1)}, s32[4]{0:T(128)}, u32[]{:S(2)}) copy-start(s32[4]{0:T(128)} %constant.60) | copy-start | bytes 52
  157.1 8.0 %collective-permute-start = (bf16[1,1,4,8,12,256]{5,3,4,2,1,0:T(8,128)(2,1)S(1)}, bf16[1,1,4,8,12,256]{5,3,4,2,1,0:T(8,128)(2,1)S(1)}, u32[]{:S(2)}, u32[]{:S(2)}) collective-permute-start(bf16[1,1,4,8,12,256]{5,3,4,2,1,0:T(8,128)(2,1)S(1)} %get-tuple-element.11), channel_id=1, source_target_pairs={{0,64},{64,128},{128,192},{192,256},{256,320},{320,384},{384,448},... | collective-permute-start | bytes 589832 | tf_op jit(solution)/shard_map/ppermute | solution.py:19
  161.5 9.0 %collective-permute-start.1 = (bf16[1,1,4,8,12,256]{5,3,4,2,1,0:T(8,128)(2,1)S(1)}, bf16[1,1,4,8,12,256]{5,3,4,2,1,0:T(8,128)(2,1)S(1)}, u32[]{:S(2)}, u32[]{:S(2)}) collective-permute-start(bf16[1,1,4,8,12,256]{5,3,4,2,1,0:T(8,128)(2,1)S(1)} %get-tuple-element.12), channel_id=1, source_target_pairs={{64,0},{128,64},{192,128},{256,192},{320,256},{384,320},{448,384},... | collective-permute-start | bytes 589832 | tf_op jit(solution)/shard_map/ppermute | solution.py:21
  163.4 19.0 %copy-start.4 = (f32[128]{0:T(128)S(1)}, f32[128]{0:T(128)}, u32[]{:S(2)}) copy-start(f32[128]{0:T(128)} %param.8) | copy-start | bytes 1540
  172.0 29.9 %collective-permute-start.2 = (bf16[1,1,24,4,12,256]{5,3,4,2,1,0:T(4,128)(2,1)}, bf16[1,1,24,4,12,256]{5,3,4,2,1,0:T(4,128)(2,1)S(1)}, u32[]{:S(2)}, u32[]{:S(2)}) collective-permute-start(bf16[1,1,24,4,12,256]{5,3,4,2,1,0:T(4,128)(2,1)} %get-tuple-element.7), channel_id=1, source_target_pairs={{0,4},{4,8},{8,12},{12,16},{16,20},{20,24},{24,28},{28,32},{32,36}... | collective-permute-start | bytes 1769480 | tf_op jit(solution)/shard_map/ppermute | solution.py:19
  176.6 30.1 %collective-permute-start.3 = (bf16[1,1,24,4,12,256]{5,3,4,2,1,0:T(4,128)(2,1)}, bf16[1,1,24,4,12,256]{5,3,4,2,1,0:T(4,128)(2,1)}, u32[]{:S(2)}, u32[]{:S(2)}) collective-permute-start(bf16[1,1,24,4,12,256]{5,3,4,2,1,0:T(4,128)(2,1)} %get-tuple-element.8), channel_id=1, source_target_pairs={{4,0},{8,4},{12,8},{16,12},{20,16},{24,20},{28,24},{32,28},{36,32}... | collective-permute-start | bytes 1769480 | tf_op jit(solution)/shard_map/ppermute | solution.py:21
  219.8 4.1 %copy-start.2 = (bf16[1,4,2,12,1,4,4,128]{7,6,5,3,2,1,4,0:T(4,128)(2,1)S(1)}, bf16[1,4,2,12,1,4,4,128]{7,6,5,3,2,1,4,0:T(4,128)(2,1)}, u32[]{:S(2)}) copy-start(bf16[1,4,2,12,1,4,4,128]{7,6,5,3,2,1,4,0:T(4,128)(2,1)} %copy.39) | copy-start | bytes 1179652
  222.2 1.7 copy-start.1
Sparse Core Ops, SparseCore 0:
  9.5 139.4 all-gather.1
where the time goes:
time: 238 us; the launch traced here: 237 us
  waiting for transfers between devices  173 us (73%)
  starting transfers between devices  16.2 us (7%)
  local copies, waits for them, and re-layouts  15.9 us (7%)
  between operations  13.7 us (6%)
  matrix products  12.1 us (5%)
  other arithmetic  7.13 us (3%)
    all_gather x1, waiting for transfers between devices, shards(): lax.all_gather(qkv_weight, 'fsdp', axis=1, tiled=True)  142 us
    ppermute x2, waiting for transfers between devices, padded_2(): lax.ppermute(tail, axis, [(i, (i + 1) % count) for i in range(count)])  20 us
    ppermute x2, waiting for transfers between devices, padded_2(): lax.ppermute(head, axis, [((i + 1) % count, i) for i in range(count)])  10.1 us
    ppermute x2, starting transfers between devices, padded_2(): lax.ppermute(tail, axis, [(i, (i + 1) % count) for i in range(count)])  8.93 us
    gather x3, local copies, waits for them, and re-layouts, attend(): chosen = jnp.take(chosen, col_pick, axis=4)  7.49 us
    ppermute x2, starting transfers between devices, padded_2(): lax.ppermute(head, axis, [((i + 1) % count, i) for i in range(count)])  7.22 us
    dot_general x1, matrix products, shards(): jnp.einsum('td,dge->tge', token_rows, lax.all_gather(qkv_weight, 'fsdp',...  7.03 us
  transfers between devices with their start and end apart: 5, of which 5 were waited for; matrix products, arithmetic and copies ran while one was open for 1% of the time, Pallas kernels for 0%

commit v1 on v0

v1 whole, which is shorter than its diff:
```python
import math

import jax
import jax.numpy as jnp
from jax import lax
from jax.experimental import pallas as pl
from jax.experimental.pallas import tpu as pltpu
from jax.sharding import PartitionSpec as P

MESH = pl.DeviceIdType.MESH
HEAD = 128
HALF = 4
LOCAL_HEADS = 3
GROUP = LOCAL_HEADS * HEAD
ROWS = 16
COLS = 8
TOKENS = ROWS * COLS
DEPTH = 1536
PIECES = ((0, 48, 0, 0), (48, 16, 1, 0), (64, 48, 0, 1), (112, 16, 1, 1))


def token_of(place):
    half, rest = place // 64, place % 64
    row = (rest // 4 + HALF) % ROWS
    return row * COLS + rest % 4 + HALF * (1 - half)


def normalized(part, gain):
    values = part.astype(jnp.float32)
    scale = lax.rsqrt(jnp.mean(values * values, axis=-1, keepdims=True) + 1e-06)
    return (values * scale * gain).astype(jnp.bfloat16)


def kernel(
    latent_hbm, weight_hbm, query_gain, key_gain, out_ref,
    latent, weight, sending, tile, blended, stage,
    load_sems, send_in, recv_in, send_twin, recv_twin, send_out, recv_out,
):
    h, w, s = lax.axis_index("ha"), lax.axis_index("wa"), lax.axis_index("fsdp")
    h_size, w_size = lax.axis_size("ha"), lax.axis_size("wa")

    def device(back_h, back_w, other):
        group = s
        if other & 1:
            group = group + 1 - 2 * lax.rem(group, 2)
        if other & 2:
            group = lax.rem(group + 2, 4)
        return (lax.rem(h - back_h + h_size, h_size), lax.rem(w - back_w + w_size, w_size), group)

    load_latent = pltpu.make_async_copy(latent_hbm, latent, load_sems.at[0])
    load_latent.start()
    load_weight = pltpu.make_async_copy(weight_hbm, weight, load_sems.at[1])
    load_weight.start()

    barrier = pltpu.get_barrier_semaphore()
    partners = [
        device(back_h, back_w, other)
        for back_h, back_w in ((0, 0), (1, 0), (0, 1), (1, 1), (-1, 0), (0, -1), (-1, -1))
        for other in range(4)
        if (back_h, back_w, other) != (0, 0, 0)
    ]
    for partner in partners:
        pl.semaphore_signal(barrier, inc=1, device_id=partner, device_id_type=MESH)

    place = lax.broadcasted_iota(jnp.int32, (TOKENS, TOKENS), 0)
    token = lax.broadcasted_iota(jnp.int32, (TOKENS, TOKENS), 1)
    arrange = jnp.where(token_of(place) == token, 1.0, 0.0).astype(jnp.bfloat16)
    place = lax.broadcasted_iota(jnp.int32, (TOKENS, TOKENS), 1)
    token = lax.broadcasted_iota(jnp.int32, (TOKENS, TOKENS), 0)
    restore = jnp.where(token_of(place) == token, 1.0, 0.0).astype(jnp.bfloat16)

    load_latent.wait()
    mine = latent[...].astype(jnp.float32).reshape(TOKENS, DEPTH).astype(jnp.bfloat16)
    sending[...] = jnp.dot(arrange, mine, preferred_element_type=jnp.float32).astype(jnp.bfloat16)
    tile[0, pl.ds(0, 48)] = sending[pl.ds(0, 48)]

    pl.semaphore_wait(barrier, len(partners))

    incoming = {}
    for slot in (0, 2):
        for index, (first, rows, back_h, back_w) in enumerate(PIECES):
            if slot == 0 and index == 0:
                continue
            at = slot * 2 + index
            copy = pltpu.make_async_remote_copy(
                src_ref=sending.at[pl.ds(first, rows)],
                dst_ref=tile.at[slot, pl.ds(first, rows)],
                send_sem=send_in.at[at],
                recv_sem=recv_in.at[at],
                device_id=device(back_h, back_w, slot),
                device_id_type=MESH,
            )
            copy.start()
            incoming[slot, index] = copy

    twin = {}

    def forward(slot, index):
        first, rows = PIECES[index][:2]
        at = slot * 2 + index
        copy = pltpu.make_async_remote_copy(
            src_ref=tile.at[slot, pl.ds(first, rows)],
            dst_ref=tile.at[slot + 1, pl.ds(first, rows)],
            send_sem=send_twin.at[at],
            recv_sem=recv_twin.at[at],
            device_id=device(0, 0, 1),
            device_id_type=MESH,
        )
        copy.start()
        twin[slot, index] = copy

    def gather(slot):
        for index in range(4):
            if (slot, index) in incoming:
                incoming[slot, index].wait_recv()
            forward(slot, index)
        for index in range(4):
            twin[slot, index].wait_recv()

    spot_q = lax.broadcasted_iota(jnp.int32, (TOKENS, TOKENS), 0)
    spot_k = lax.broadcasted_iota(jnp.int32, (TOKENS, TOKENS), 1)
    together = (spot_q % 64 < 32) == (spot_k % 64 < 32)

    outgoing = {}

    def attend(slot):
        tokens = jnp.concatenate([tile[slot], tile[slot + 1]], axis=0)
        for head in range(LOCAL_HEADS):
            packed = jnp.dot(tokens, weight[head], preferred_element_type=jnp.float32).astype(jnp.bfloat16)
            queries = normalized(packed[:, :HEAD], query_gain[...])
            keyed = normalized(packed[:, HEAD : 2 * HEAD], key_gain[...])
            valued = packed[:, 2 * HEAD :]
            for clip in range(2):
                at = slice(clip * TOKENS, (clip + 1) * TOKENS)
                scores = lax.dot_general(
                    queries[at], keyed[at], (((1,), (1,)), ((), ())), preferred_element_type=jnp.float32
                ) * (1.0 / math.sqrt(HEAD))
                scores = jnp.where(together, scores, -1e30)
                raised = jnp.exp(scores - jnp.max(scores, axis=-1, keepdims=True))
                probs = (raised / jnp.sum(raised, axis=-1, keepdims=True)).astype(jnp.bfloat16)
                result = jnp.dot(probs, valued[at], preferred_element_type=jnp.float32)
                blended[slot + clip, :, pl.ds(head * HEAD, HEAD)] = result.astype(jnp.bfloat16)
        for clip in (slot, slot + 1):
            for index, (first, rows, back_h, back_w) in enumerate(PIECES):
                if clip == 0 and index == 0:
                    stage[0, pl.ds(0, 48)] = blended[0, pl.ds(0, 48)]
                    continue
                at = clip * 4 + index
                copy = pltpu.make_async_remote_copy(
                    src_ref=blended.at[clip, pl.ds(first, rows)],
                    dst_ref=stage.at[clip, pl.ds(first, rows)],
                    send_sem=send_out.at[at],
                    recv_sem=recv_out.at[at],
                    device_id=device(-back_h, -back_w, clip),
                    device_id_type=MESH,
                )
                copy.start()
                outgoing[clip, index] = copy

    gather(0)
    load_weight.wait()
    attend(0)
    gather(2)
    attend(2)

    for clip in range(4):
        for index in range(4):
            if (clip, index) in outgoing:
                outgoing[clip, index].wait_recv()
        group = device(0, 0, clip)[2]
        columns = pl.ds(pl.multiple_of(group * GROUP, GROUP), GROUP)
        out_ref[:, columns] = jnp.dot(restore, stage[clip], preferred_element_type=jnp.float32).astype(jnp.bfloat16)
    for copy in [*incoming.values(), *twin.values(), *outgoing.values()]:
        copy.wait_send()


def shards(latent, qkv_weight, query_gain, key_gain):
    vmem = pl.BlockSpec(memory_space=pltpu.VMEM)
    anywhere = pl.BlockSpec(memory_space=pl.ANY)
    out = pl.pallas_call(
        kernel,
        out_shape=jax.ShapeDtypeStruct((TOKENS, DEPTH), jnp.bfloat16),
        in_specs=[anywhere, anywhere, vmem, vmem],
        out_specs=vmem,
        scratch_shapes=[
            pltpu.VMEM((ROWS, COLS, DEPTH), jnp.bfloat16),
            pltpu.VMEM((LOCAL_HEADS, DEPTH, GROUP), jnp.bfloat16),
            pltpu.VMEM((TOKENS, DEPTH), jnp.bfloat16),
            pltpu.VMEM((4, TOKENS, DEPTH), jnp.bfloat16),
            pltpu.VMEM((4, TOKENS, GROUP), jnp.bfloat16),
            pltpu.VMEM((4, TOKENS, GROUP), jnp.bfloat16),
            pltpu.SemaphoreType.DMA((2,)),
            pltpu.SemaphoreType.DMA((8,)),
            pltpu.SemaphoreType.DMA((8,)),
            pltpu.SemaphoreType.DMA((8,)),
            pltpu.SemaphoreType.DMA((8,)),
            pltpu.SemaphoreType.DMA((16,)),
            pltpu.SemaphoreType.DMA((16,)),
        ],
        compiler_params=pltpu.CompilerParams(
            collective_id=0, has_side_effects=True, vmem_limit_bytes=60 * 1024 * 1024
        ),
    )(
        latent.reshape(ROWS, COLS, DEPTH),
        qkv_weight.transpose(1, 0, 2),
        query_gain.reshape(1, HEAD),
        key_gain.reshape(1, HEAD),
    )
    return out.reshape(latent.shape)


def solution(mesh):
    return jax.shard_map(
        shards,
        mesh=mesh,
        in_specs=(P("fsdp", None, "ha", "wa", None), P(None, "fsdp", None), P(), P()),
        out_specs=P("fsdp", None, "ha", "wa", None),
        check_vma=False,
    )
```

time: 238 us -> 45 us (0.19)
  the two profiles are of different devices: /device:TPU:25 before, /device:TPU:1 now
where the time goes in v1:
time: 45 us; the launch traced here: 44.9 us
  Pallas kernels  43.1 us (96%)
  local copies, waits for them, and re-layouts  1.77 us (4%)
    pallas_call x1, Pallas kernels, shards(): pl.pallas_call(kernel, out_shape=jax.ShapeDtypeStruct((TOKENS, DEPTH), jn...  43.1 us
    unnamed x1, local copies, waits for them, and re-layouts  1.77 us

profile of v1, /device:TPU:1, one launch (start us, length us, event | category | flops | bytes accessed | tf_op | source)
XLA Modules:
  0.0 44.9 jit_solution(11768440208406817481)
XLA Ops:
  0.0 43.1 %shard_map.46 = bf16[128,1536]{1,0:T(8,128)(2,1)} custom-call(bf16[16,8,1536]{2,1,0:T(8,128)(2,1)} %bitcast.7, bf16[3,1536,384]{2,1,0:T(8,128)(2,1)} %bitcast.5, f32[1,128]{1,0:T(1,128)} %bitcast.8, f32[1,128]{1,0:T(1,128)} %bitcast.9), custom_call_target="tpu_custom_call" | custom-call | tf_op jit(solution)/shard_map/pallas_call | solution.py:180
  43.1 1.8 %copy.6 = bf16[1,1,16,8,1536]{4,3,2,1,0:T(8,128)(2,1)} copy(bf16[1,1,16,8,1536]{4,3,2,1,0:T(8,128)(2,1)} %bitcast.6) | data formatting | bytes 786432

commit v2 on v1

v2 whole, which is shorter than its diff:
```python
import math

import jax
import jax.numpy as jnp
from jax import lax
from jax.experimental import pallas as pl
from jax.experimental.pallas import tpu as pltpu
from jax.sharding import PartitionSpec as P

MESH = pl.DeviceIdType.MESH
HEAD = 128
HALF = 4
LOCAL_HEADS = 3
GROUP = LOCAL_HEADS * HEAD
ROWS = 16
COLS = 8
TOKENS = ROWS * COLS
DEPTH = 1536
PIECES = ((0, 48, 0, 1), (48, 16, -1, 1), (64, 48, 0, 0), (112, 16, -1, 0))
STAYS = 2


def token_of(place):
    half, rest = place // 64, place % 64
    row = (rest // 4 + HALF) % ROWS
    return row * COLS + rest % 4 + HALF * (1 - half)


def normalized(part, gain):
    values = part.astype(jnp.float32)
    scale = lax.rsqrt(jnp.mean(values * values, axis=-1, keepdims=True) + 1e-06)
    return (values * scale * gain).astype(jnp.bfloat16)


def kernel(
    latent_hbm, weight_hbm, query_gain_hbm, key_gain_hbm, out_ref,
    latent, weight, query_gain, key_gain, sending, tile, blended, stage,
    load_sems, send_in, recv_in, send_twin, recv_twin, send_out, recv_out,
):
    h, w, s = lax.axis_index("ha"), lax.axis_index("wa"), lax.axis_index("fsdp")
    h_size, w_size = lax.axis_size("ha"), lax.axis_size("wa")

    def device(on_h, on_w, other):
        group = s
        if other & 1:
            group = group + 1 - 2 * lax.rem(group, 2)
        if other & 2:
            group = lax.rem(group + 2, 4)
        return (lax.rem(h + on_h + h_size, h_size), lax.rem(w + on_w + w_size, w_size), group)

    barrier = pltpu.get_barrier_semaphore()
    givers = [device(0, 0, 1)]
    for slot in (0, 2):
        for index, (_, _, on_h, on_w) in enumerate(PIECES):
            if (slot, index) != (0, STAYS):
                givers.append(device(-on_h, -on_w, slot))
    for giver in givers:
        pl.semaphore_signal(barrier, inc=1, device_id=giver, device_id_type=MESH)

    load_latent = pltpu.make_async_copy(latent_hbm, latent, load_sems.at[0])
    load_latent.start()
    loads = [
        pltpu.make_async_copy(source, target, load_sems.at[1 + at])
        for at, (source, target) in enumerate(
            ((query_gain_hbm, query_gain), (key_gain_hbm, key_gain), (weight_hbm, weight))
        )
    ]
    for load in loads:
        load.start()

    place = lax.broadcasted_iota(jnp.int32, (TOKENS, TOKENS), 0)
    token = lax.broadcasted_iota(jnp.int32, (TOKENS, TOKENS), 1)
    arrange = jnp.where(token_of(place) == token, 1.0, 0.0).astype(jnp.bfloat16)

    load_latent.wait()
    mine = latent[...].astype(jnp.float32).reshape(TOKENS, DEPTH).astype(jnp.bfloat16)
    sending[...] = jnp.dot(arrange, mine, preferred_element_type=jnp.float32).astype(jnp.bfloat16)

    pl.semaphore_wait(barrier, len(givers))

    incoming = {}
    for slot, index in ((0, 0), (0, 1), (2, 0), (2, 1), (0, 3), (2, 2), (2, 3)):
        first, rows, on_h, on_w = PIECES[index]
        at = slot * 2 + index
        copy = pltpu.make_async_remote_copy(
            src_ref=sending.at[pl.ds(first, rows)],
            dst_ref=tile.at[slot, pl.ds(first, rows)],
            send_sem=send_in.at[at],
            recv_sem=recv_in.at[at],
            device_id=device(on_h, on_w, slot),
            device_id_type=MESH,
        )
        copy.start()
        incoming[slot, index] = copy
    stays = pl.ds(PIECES[STAYS][0], PIECES[STAYS][1])
    tile[0, stays] = sending[stays]

    twin = {}

    def forward(slot):
        for index in (2, 3, 1, 0):
            first, rows = PIECES[index][:2]
            at = slot * 2 + index
            if (slot, index) in incoming:
                incoming[slot, index].wait_recv()
            copy = pltpu.make_async_remote_copy(
                src_ref=tile.at[slot, pl.ds(first, rows)],
                dst_ref=tile.at[slot + 1, pl.ds(first, rows)],
                send_sem=send_twin.at[at],
                recv_sem=recv_twin.at[at],
                device_id=device(0, 0, 1),
                device_id_type=MESH,
            )
            copy.start()
            twin[slot, index] = copy

    spot_q = lax.broadcasted_iota(jnp.int32, (TOKENS, TOKENS), 0)
    spot_k = lax.broadcasted_iota(jnp.int32, (TOKENS, TOKENS), 1)
    together = (spot_q % 64 < 32) == (spot_k % 64 < 32)

    outgoing = {}

    def attend(slot):
        tokens = tile[slot]
        for head in range(LOCAL_HEADS):
            packed = jnp.dot(tokens, weight[head], preferred_element_type=jnp.float32).astype(jnp.bfloat16)
            queries = normalized(packed[:, :HEAD], query_gain[...])
            keyed = normalized(packed[:, HEAD : 2 * HEAD], key_gain[...])
            scores = lax.dot_general(
                queries, keyed, (((1,), (1,)), ((), ())), preferred_element_type=jnp.float32
            ) * (1.0 / math.sqrt(HEAD))
            raised = jnp.exp(jnp.where(together, scores, -1e30))
            result = jnp.dot(
                raised.astype(jnp.bfloat16), packed[:, 2 * HEAD :], preferred_element_type=jnp.float32
            ) / jnp.sum(raised, axis=-1, keepdims=True)
            blended[slot, :, pl.ds(head * HEAD, HEAD)] = result.astype(jnp.bfloat16)
        for index, (first, rows, on_h, on_w) in enumerate(PIECES):
            if (slot, index) == (0, STAYS):
                stage[0, stays] = blended[0, stays]
                continue
            at = slot * 4 + index
            copy = pltpu.make_async_remote_copy(
                src_ref=blended.at[slot, pl.ds(first, rows)],
                dst_ref=stage.at[slot, pl.ds(first, rows)],
                send_sem=send_out.at[at],
                recv_sem=recv_out.at[at],
                device_id=device(-on_h, -on_w, slot),
                device_id_type=MESH,
            )
            copy.start()
            outgoing[slot, index] = copy

    forward(0)
    for load in loads:
        load.wait()
    attend(0)
    for index in range(4):
        twin[0, index].wait_recv()
    attend(1)
    forward(2)
    attend(2)
    for index in range(4):
        twin[2, index].wait_recv()
    attend(3)

    place = lax.broadcasted_iota(jnp.int32, (TOKENS, TOKENS), 1)
    token = lax.broadcasted_iota(jnp.int32, (TOKENS, TOKENS), 0)
    restore = jnp.where(token_of(place) == token, 1.0, 0.0).astype(jnp.bfloat16)
    for slot in range(4):
        for index in range(4):
            if (slot, index) in outgoing:
                outgoing[slot, index].wait_recv()
        columns = pl.ds(pl.multiple_of(device(0, 0, slot)[2] * GROUP, GROUP), GROUP)
        out_ref[:, columns] = jnp.dot(restore, stage[slot], preferred_element_type=jnp.float32).astype(jnp.bfloat16)
    for copy in [*incoming.values(), *twin.values(), *outgoing.values()]:
        copy.wait_send()


def shards(latent, qkv_weight, query_gain, key_gain):
    vmem = pl.BlockSpec(memory_space=pltpu.VMEM)
    anywhere = pl.BlockSpec(memory_space=pltpu.HBM)
    out = pl.pallas_call(
        kernel,
        out_shape=pltpu.VMEM((TOKENS, DEPTH), jnp.bfloat16),
        in_specs=[anywhere] * 4,
        out_specs=vmem,
        scratch_shapes=[
            pltpu.VMEM((ROWS, COLS, DEPTH), jnp.bfloat16),
            pltpu.VMEM((LOCAL_HEADS, DEPTH, GROUP), jnp.bfloat16),
            pltpu.VMEM((1, HEAD), jnp.float32),
            pltpu.VMEM((1, HEAD), jnp.float32),
            pltpu.VMEM((TOKENS, DEPTH), jnp.bfloat16),
            pltpu.VMEM((4, TOKENS, DEPTH), jnp.bfloat16),
            pltpu.VMEM((4, TOKENS, GROUP), jnp.bfloat16),
            pltpu.VMEM((4, TOKENS, GROUP), jnp.bfloat16),
            pltpu.SemaphoreType.DMA((4,)),
            pltpu.SemaphoreType.DMA((8,)),
            pltpu.SemaphoreType.DMA((8,)),
            pltpu.SemaphoreType.DMA((8,)),
            pltpu.SemaphoreType.DMA((8,)),
            pltpu.SemaphoreType.DMA((16,)),
            pltpu.SemaphoreType.DMA((16,)),
        ],
        compiler_params=pltpu.CompilerParams(
            collective_id=0, has_side_effects=True, vmem_limit_bytes=60 * 1024 * 1024
        ),
    )(
        latent.reshape(ROWS, COLS, DEPTH),
        qkv_weight.transpose(1, 0, 2),
        query_gain.reshape(1, HEAD),
        key_gain.reshape(1, HEAD),
    )
    return out.reshape(latent.shape)


def solution(mesh):
    return jax.shard_map(
        shards,
        mesh=mesh,
        in_specs=(P("fsdp", None, "ha", "wa", None), P(None, "fsdp", None), P(), P()),
        out_specs=P("fsdp", None, "ha", "wa", None),
        check_vma=False,
    )
```

time: 45 us -> 36.9 us (0.82)
  Pallas kernels: 43.1 us -> 36.1 us
  local copies, waits for them, and re-layouts: 1.77 us -> 0.75 us
    pallas_call x1, Pallas kernels: 43.1 us -> 36.1 us  [shards(): pl.pallas_call(kernel, out_shape=pltpu.VMEM((TOKENS, DEPTH), jnp.bfloat16...]
    unnamed x1, local copies, waits for them, and re-layouts: 1.77 us -> 0.75 us
where the time goes in v2:
time: 36.9 us; the launch traced here: 36.8 us
  Pallas kernels  36.1 us (98%)
  local copies, waits for them, and re-layouts  0.75 us (2%)
    pallas_call x1, Pallas kernels, shards(): pl.pallas_call(kernel, out_shape=pltpu.VMEM((TOKENS, DEPTH), jnp.bfloat16...  36.1 us
    unnamed x1, local copies, waits for them, and re-layouts  0.75 us

profile of v2, /device:TPU:1, one launch (start us, length us, event | category | flops | bytes accessed | tf_op | source)
XLA Modules:
  0.0 36.8 jit_solution(6192753796127600904)
XLA Ops:
  0.0 36.1 %shard_map.46 = bf16[128,1536]{1,0:T(8,128)(2,1)S(1)} custom-call(bf16[16,8,1536]{2,1,0:T(8,128)(2,1)} %bitcast.7, bf16[3,1536,384]{2,1,0:T(8,128)(2,1)} %bitcast.6, f32[1,128]{1,0:T(1,128)} %bitcast.8, f32[1,128]{1,0:T(1,128)} %bitcast.9), custom_call_target="tpu_custom_call" | custom-call | tf_op jit(solution)/shard_map/pallas_call | solution.py:182
  36.1 0.7 %copy.6 = bf16[1,1,16,8,1536]{4,3,2,1,0:T(8,128)(2,1)} copy(bf16[1,1,16,8,1536]{4,3,2,1,0:T(8,128)(2,1)S(1)} %bitcast.5) | data formatting | bytes 786432

commit v3 on v2

v3 whole, which is shorter than its diff:
```python
import math

import jax
import jax.numpy as jnp
from jax import lax
from jax.experimental import pallas as pl
from jax.experimental.pallas import tpu as pltpu
from jax.sharding import PartitionSpec as P

MESH = pl.DeviceIdType.MESH
HEAD = 128
HALF = 4
LOCAL_HEADS = 3
GROUP = LOCAL_HEADS * HEAD
ROWS = 16
COLS = 8
TOKENS = ROWS * COLS
DEPTH = 1536
R_MAIN, R_TOP, L_MAIN, L_TOP = (0, 48, 0, 1), (48, 16, -1, 1), (64, 48, 0, 0), (112, 16, -1, 0)
PIECES = (R_TOP, R_MAIN, L_TOP, L_MAIN)
COPIES = 26
CHUNKS = ((0, 16, 0, 1), (16, 16, 0, 1), (32, 16, 0, 1), R_TOP)


def token_of(place):
    half, rest = place // 64, place % 64
    row = (rest // 4 + HALF) % ROWS
    return row * COLS + rest % 4 + HALF * (1 - half)


def normalized(part, gain):
    values = part.astype(jnp.float32)
    scale = lax.rsqrt(jnp.mean(values * values, axis=-1, keepdims=True) + 1e-06)
    return (values * scale * gain).astype(jnp.bfloat16)


def kernel(
    latent_hbm, weight_hbm, query_gain_hbm, key_gain_hbm, out_ref,
    latent, weight, query_gain, key_gain, sending, tile, blended, stage,
    load_sems, send_sems, recv_sems,
):
    h, w, s = lax.axis_index("ha"), lax.axis_index("wa"), lax.axis_index("fsdp")
    h_size, w_size = lax.axis_size("ha"), lax.axis_size("wa")

    known = {}

    def device(on_h, on_w, other):
        key = (on_h, on_w, other)
        if key not in known:
            known[key] = locate(*key)
        return known[key]

    def locate(on_h, on_w, other):
        group = s
        if other & 1:
            group = group + 1 - 2 * lax.rem(group, 2)
        if other & 2:
            group = lax.rem(group + 2, 4)
        return (lax.rem(h + on_h + h_size, h_size), lax.rem(w + on_w + w_size, w_size), group)

    load_latent = pltpu.make_async_copy(latent_hbm, latent, load_sems.at[0])
    load_latent.start()

    barrier = pltpu.get_barrier_semaphore()
    givers = [device(0, 0, 1), device(0, 0, 2), device(0, -1, 2), device(1, -1, 2), device(1, 0, 0), device(1, 0, 2)]
    for giver in givers:
        pl.semaphore_signal(barrier, inc=1, device_id=giver, device_id_type=MESH)

    moves = [(query_gain_hbm, query_gain), (key_gain_hbm, key_gain)]
    for head in range(LOCAL_HEADS):
        both, value = pl.ds(2 * HEAD * head, 2 * HEAD), pl.ds(HEAD * (2 * LOCAL_HEADS + head), HEAD)
        moves.append((weight_hbm.at[head, :, pl.ds(0, 2 * HEAD)], weight.at[0, :, both]))
        moves.append((weight_hbm.at[head, :, pl.ds(2 * HEAD, HEAD)], weight.at[0, :, value]))
    loads = [
        pltpu.make_async_copy(source, target, load_sems.at[1 + at]) for at, (source, target) in enumerate(moves)
    ]

    place = lax.broadcasted_iota(jnp.int32, (TOKENS, TOKENS), 0)
    token = lax.broadcasted_iota(jnp.int32, (TOKENS, TOKENS), 1)
    arrange = jnp.where(token_of(place) == token, 1.0, 0.0).astype(jnp.bfloat16)

    load_latent.wait()
    for load in loads:
        load.start()
    mine = latent[...].astype(jnp.float32).reshape(TOKENS, DEPTH).astype(jnp.bfloat16)
    right, left = pl.ds(0, 64), pl.ds(64, 64)
    sending[right] = jnp.dot(arrange[:64], mine, preferred_element_type=jnp.float32).astype(jnp.bfloat16)

    pl.semaphore_wait(barrier, len(givers))

    copies = []

    def send(source, target, rows, to):
        number = len(copies)
        copy = pltpu.make_async_remote_copy(
            src_ref=source.at[rows],
            dst_ref=target.at[rows],
            send_sem=send_sems.at[number],
            recv_sem=recv_sems.at[number],
            device_id=to,
            device_id_type=MESH,
        )
        copy.start()
        copies.append(copy)
        return copy

    def rows_of(piece):
        return pl.ds(piece[0], piece[1])

    right_in = [
        send(sending, tile.at[1], rows_of(chunk), device(chunk[2], chunk[3], 2))
        for chunk in (CHUNKS[3], CHUNKS[0], CHUNKS[1], CHUNKS[2])
    ]
    right_in = [*right_in[1:], right_in[0]]
    sending[left] = jnp.dot(arrange[64:], mine, preferred_element_type=jnp.float32).astype(jnp.bfloat16)
    left_in = [
        send(sending, tile.at[0], rows_of(L_TOP), device(-1, 0, 0)),
        send(sending, tile.at[1], rows_of(L_TOP), device(-1, 0, 2)),
        send(sending, tile.at[1], rows_of(L_MAIN), device(0, 0, 2)),
    ]
    tile[0, rows_of(L_MAIN)] = sending[rows_of(L_MAIN)]

    for load in loads:
        load.wait()
    weight_in = send(weight.at[0], weight.at[1], pl.ds(0, DEPTH), device(0, 0, 1))

    relayed = []
    for chunk, copy in zip(CHUNKS, right_in):
        copy.wait_recv()
        relayed.append(send(tile.at[1], tile.at[0], rows_of(chunk), device(0, 0, 2)))
    for copy in left_in:
        copy.wait_recv()

    spot_q = lax.broadcasted_iota(jnp.int32, (TOKENS, TOKENS), 0)
    spot_k = lax.broadcasted_iota(jnp.int32, (TOKENS, TOKENS), 1)
    together = (spot_q % 64 < 32) == (spot_k % 64 < 32)

    outgoing = {}

    def attend(slot, part):
        tokens = tile[slot]
        raised = []
        for head in range(LOCAL_HEADS):
            both = weight[part, :, 2 * HEAD * head : 2 * HEAD * (head + 1)]
            packed = jnp.dot(tokens, both, preferred_element_type=jnp.float32).astype(jnp.bfloat16)
            queries = normalized(packed[:, :HEAD], query_gain[...])
            keyed = normalized(packed[:, HEAD:], key_gain[...])
            scores = lax.dot_general(
                queries, keyed, (((1,), (1,)), ((), ())), preferred_element_type=jnp.float32
            ) * (1.0 / math.sqrt(HEAD))
            raised.append(jnp.exp(jnp.where(together, scores, -1e30)))
        values = weight[part, :, 2 * HEAD * LOCAL_HEADS :]
        valued = jnp.dot(tokens, values, preferred_element_type=jnp.float32).astype(jnp.bfloat16)
        for head in range(LOCAL_HEADS):
            columns = slice(head * HEAD, (head + 1) * HEAD)
            result = jnp.dot(
                raised[head].astype(jnp.bfloat16), valued[:, columns], preferred_element_type=jnp.float32
            ) / jnp.sum(raised[head], axis=-1, keepdims=True)
            blended[slot, part, :, columns] = result.astype(jnp.bfloat16)
        outgoing[slot, part] = []
        for piece in PIECES:
            rows = rows_of(piece)
            if slot == 0 and piece == L_MAIN:
                stage[0, part, rows] = blended[0, part, rows]
            else:
                to = device(-piece[2], -piece[3], 2 * slot)
                outgoing[slot, part].append(send(blended.at[slot, part], stage.at[slot, part], rows, to))

    attend(1, 0)
    weight_in.wait_recv()
    attend(1, 1)
    for copy in relayed:
        copy.wait_recv()
    attend(0, 0)
    attend(0, 1)

    place = lax.broadcasted_iota(jnp.int32, (TOKENS, TOKENS), 1)
    token = lax.broadcasted_iota(jnp.int32, (TOKENS, TOKENS), 0)
    restore = jnp.where(token_of(place) == token, 1.0, 0.0).astype(jnp.bfloat16)
    for slot, part in ((1, 0), (1, 1), (0, 0), (0, 1)):
        for copy in outgoing[slot, part]:
            copy.wait_recv()
        columns = pl.ds(pl.multiple_of(device(0, 0, 2 * slot + part)[2] * GROUP, GROUP), GROUP)
        rebuilt = jnp.dot(restore, stage[slot, part], preferred_element_type=jnp.float32)
        out_ref[:, columns] = rebuilt.astype(jnp.bfloat16)
    for copy in copies:
        copy.wait_send()


def shards(latent, qkv_weight, query_gain, key_gain):
    vmem = pl.BlockSpec(memory_space=pltpu.VMEM)
    anywhere = pl.BlockSpec(memory_space=pltpu.HBM)
    out = pl.pallas_call(
        kernel,
        out_shape=pltpu.VMEM((TOKENS, DEPTH), jnp.bfloat16),
        in_specs=[anywhere] * 4,
        out_specs=vmem,
        scratch_shapes=[
            pltpu.VMEM((ROWS, COLS, DEPTH), jnp.bfloat16),
            pltpu.VMEM((2, DEPTH, LOCAL_HEADS * GROUP), jnp.bfloat16),
            pltpu.VMEM((1, HEAD), jnp.float32),
            pltpu.VMEM((1, HEAD), jnp.float32),
            pltpu.VMEM((TOKENS, DEPTH), jnp.bfloat16),
            pltpu.VMEM((2, TOKENS, DEPTH), jnp.bfloat16),
            pltpu.VMEM((2, 2, TOKENS, GROUP), jnp.bfloat16),
            pltpu.VMEM((2, 2, TOKENS, GROUP), jnp.bfloat16),
            pltpu.SemaphoreType.DMA((9,)),
            pltpu.SemaphoreType.DMA((COPIES,)),
            pltpu.SemaphoreType.DMA((COPIES,)),
        ],
        compiler_params=pltpu.CompilerParams(
            collective_id=0, has_side_effects=True, vmem_limit_bytes=60 * 1024 * 1024
        ),
    )(
        latent.reshape(ROWS, COLS, DEPTH),
        qkv_weight.transpose(1, 0, 2),
        query_gain.reshape(1, HEAD),
        key_gain.reshape(1, HEAD),
    )
    return out.reshape(latent.shape)


def solution(mesh):
    return jax.shard_map(
        shards,
        mesh=mesh,
        in_specs=(P("fsdp", None, "ha", "wa", None), P(None, "fsdp", None), P(), P()),
        out_specs=P("fsdp", None, "ha", "wa", None),
        check_vma=False,
    )
```

time: 36.9 us -> 35.1 us (0.951)
  the two profiles are of different devices: /device:TPU:1 before, /device:TPU:2 now
where the time goes in v3:
time: 35.1 us; the launch traced here: 34.9 us
  Pallas kernels  34.2 us (97%)
  local copies, waits for them, and re-layouts  0.75 us (2%)
    pallas_call x1, Pallas kernels, shards(): pl.pallas_call(kernel, out_shape=pltpu.VMEM((TOKENS, DEPTH), jnp.bfloat16...  34.2 us
    unnamed x1, local copies, waits for them, and re-layouts  0.75 us

profile of v3, /device:TPU:2, one launch (start us, length us, event | category | flops | bytes accessed | tf_op | source)
XLA Modules:
  0.0 34.9 jit_solution(12765869010450594660)
XLA Ops:
  0.0 34.2 %shard_map.46 = bf16[128,1536]{1,0:T(8,128)(2,1)S(1)} custom-call(bf16[16,8,1536]{2,1,0:T(8,128)(2,1)} %bitcast.7, bf16[3,1536,384]{2,1,0:T(8,128)(2,1)} %bitcast.6, f32[1,128]{1,0:T(1,128)} %bitcast.8, f32[1,128]{1,0:T(1,128)} %bitcast.9), custom_call_target="tpu_custom_call" | custom-call | tf_op jit(solution)/shard_map/pallas_call | solution.py:193
  34.2 0.7 %copy.6 = bf16[1,1,16,8,1536]{4,3,2,1,0:T(8,128)(2,1)} copy(bf16[1,1,16,8,1536]{4,3,2,1,0:T(8,128)(2,1)S(1)} %bitcast.5) | data formatting | bytes 786432

commit v4 on v3

--- a/solution.py
+++ b/solution.py
@@ -17,8 +17,8 @@
 TOKENS = ROWS * COLS
 DEPTH = 1536
 R_MAIN, R_TOP, L_MAIN, L_TOP = (0, 48, 0, 1), (48, 16, -1, 1), (64, 48, 0, 0), (112, 16, -1, 0)
-PIECES = (R_TOP, R_MAIN, L_TOP, L_MAIN)
-COPIES = 26
+PIECES = (L_TOP, L_MAIN, R_TOP, R_MAIN)
+COPIES = 19
 CHUNKS = ((0, 16, 0, 1), (16, 16, 0, 1), (32, 16, 0, 1), R_TOP)
 
 
@@ -137,52 +137,53 @@
 
     outgoing = {}
 
-    def attend(slot, part):
+    def attend(slot):
         tokens = tile[slot]
-        raised = []
-        for head in range(LOCAL_HEADS):
-            both = weight[part, :, 2 * HEAD * head : 2 * HEAD * (head + 1)]
-            packed = jnp.dot(tokens, both, preferred_element_type=jnp.float32).astype(jnp.bfloat16)
-            queries = normalized(packed[:, :HEAD], query_gain[...])
-            keyed = normalized(packed[:, HEAD:], key_gain[...])
-            scores = lax.dot_general(
-                queries, keyed, (((1,), (1,)), ((), ())), preferred_element_type=jnp.float32
-            ) * (1.0 / math.sqrt(HEAD))
-            raised.append(jnp.exp(jnp.where(together, scores, -1e30)))
-        values = weight[part, :, 2 * HEAD * LOCAL_HEADS :]
-        valued = jnp.dot(tokens, values, preferred_element_type=jnp.float32).astype(jnp.bfloat16)
-        for head in range(LOCAL_HEADS):
-            columns = slice(head * HEAD, (head + 1) * HEAD)
-            result = jnp.dot(
-                raised[head].astype(jnp.bfloat16), valued[:, columns], preferred_element_type=jnp.float32
-            ) / jnp.sum(raised[head], axis=-1, keepdims=True)
-            blended[slot, part, :, columns] = result.astype(jnp.bfloat16)
-        outgoing[slot, part] = []
+        raised = {}
+        for part in range(2):
+            for head in range(LOCAL_HEADS):
+                both = weight[part, :, 2 * HEAD * head : 2 * HEAD * (head + 1)]
+                packed = jnp.dot(tokens, both, preferred_element_type=jnp.float32).astype(jnp.bfloat16)
+                queries = normalized(packed[:, :HEAD], query_gain[...])
+                keyed = normalized(packed[:, HEAD:], key_gain[...])
+                scores = lax.dot_general(
+                    queries, keyed, (((1,), (1,)), ((), ())), preferred_element_type=jnp.float32
+                ) * (1.0 / math.sqrt(HEAD))
+                raised[part, head] = jnp.exp(jnp.where(together, scores, -1e30))
+        for part in range(2):
+            values = weight[part, :, 2 * HEAD * LOCAL_HEADS :]
+            valued = jnp.dot(tokens, values, preferred_element_type=jnp.float32).astype(jnp.bfloat16)
+            for head in range(LOCAL_HEADS):
+                columns = slice(head * HEAD, (head + 1) * HEAD)
+                result = jnp.dot(
+                    raised[part, head].astype(jnp.bfloat16), valued[:, columns], preferred_element_type=jnp.float32
+                ) / jnp.sum(raised[part, head], axis=-1, keepdims=True)
+                blended[slot, :, pl.ds(part * GROUP + head * HEAD, HEAD)] = result.astype(jnp.bfloat16)
+        outgoing[slot] = []
         for piece in PIECES:
             rows = rows_of(piece)
             if slot == 0 and piece == L_MAIN:
-                stage[0, part, rows] = blended[0, part, rows]
+                stage[0, rows] = blended[0, rows]
             else:
                 to = device(-piece[2], -piece[3], 2 * slot)
-                outgoing[slot, part].append(send(blended.at[slot, part], stage.at[slot, part], rows, to))
-
-    attend(1, 0)
+                outgoing[slot].append(send(blended.at[slot], stage.at[slot], rows, to))
+
     weight_in.wait_recv()
-    attend(1, 1)
+    attend(1)
     for copy in relayed:
         copy.wait_recv()
-    attend(0, 0)
-    attend(0, 1)
+    attend(0)
 
     place = lax.broadcasted_iota(jnp.int32, (TOKENS, TOKENS), 1)
     token = lax.broadcasted_iota(jnp.int32, (TOKENS, TOKENS), 0)
     restore = jnp.where(token_of(place) == token, 1.0, 0.0).astype(jnp.bfloat16)
-    for slot, part in ((1, 0), (1, 1), (0, 0), (0, 1)):
-        for copy in outgoing[slot, part]:
+    for slot in (1, 0):
+        for copy in outgoing[slot]:
             copy.wait_recv()
-        columns = pl.ds(pl.multiple_of(device(0, 0, 2 * slot + part)[2] * GROUP, GROUP), GROUP)
-        rebuilt = jnp.dot(restore, stage[slot, part], preferred_element_type=jnp.float32)
-        out_ref[:, columns] = rebuilt.astype(jnp.bfloat16)
+        rebuilt = jnp.dot(restore, stage[slot], preferred_element_type=jnp.float32).astype(jnp.bfloat16)
+        for part in range(2):
+            columns = pl.ds(pl.multiple_of(device(0, 0, 2 * slot + part)[2] * GROUP, GROUP), GROUP)
+            out_ref[:, columns] = rebuilt[:, part * GROUP : (part + 1) * GROUP]
     for copy in copies:
         copy.wait_send()
 
@@ -202,8 +203,8 @@
             pltpu.VMEM((1, HEAD), jnp.float32),
             pltpu.VMEM((TOKENS, DEPTH), jnp.bfloat16),
             pltpu.VMEM((2, TOKENS, DEPTH), jnp.bfloat16),
-            pltpu.VMEM((2, 2, TOKENS, GROUP), jnp.bfloat16),
-            pltpu.VMEM((2, 2, TOKENS, GROUP), jnp.bfloat16),
+            pltpu.VMEM((2, TOKENS, 2 * GROUP), jnp.bfloat16),
+            pltpu.VMEM((2, TOKENS, 2 * GROUP), jnp.bfloat16),
             pltpu.SemaphoreType.DMA((9,)),
             pltpu.SemaphoreType.DMA((COPIES,)),
             pltpu.SemaphoreType.DMA((COPIES,)),

time: 35.1 us -> 34.4 us (0.980)
  Pallas kernels: 34.2 us -> 33.5 us
    pallas_call x1, Pallas kernels: 34.2 us -> 33.5 us  [shards(): pl.pallas_call(kernel, out_shape=pltpu.VMEM((TOKENS, DEPTH), jnp.bfloat16...]
where the time goes in v4:
time: 34.4 us; the launch traced here: 34.3 us
  Pallas kernels  33.5 us (97%)
  local copies, waits for them, and re-layouts  0.75 us (2%)
    pallas_call x1, Pallas kernels, shards(): pl.pallas_call(kernel, out_shape=pltpu.VMEM((TOKENS, DEPTH), jnp.bfloat16...  33.5 us
    unnamed x1, local copies, waits for them, and re-layouts  0.75 us

profile of v4, /device:TPU:2, one launch (start us, length us, event | category | flops | bytes accessed | tf_op | source)
XLA Modules:
  0.0 34.3 jit_solution(10386888099546675911)
XLA Ops:
  0.0 33.5 %shard_map.46 = bf16[128,1536]{1,0:T(8,128)(2,1)S(1)} custom-call(bf16[16,8,1536]{2,1,0:T(8,128)(2,1)} %bitcast.7, bf16[3,1536,384]{2,1,0:T(8,128)(2,1)} %bitcast.6, f32[1,128]{1,0:T(1,128)} %bitcast.8, f32[1,128]{1,0:T(1,128)} %bitcast.9), custom_call_target="tpu_custom_call" | custom-call | tf_op jit(solution)/shard_map/pallas_call | solution.py:194
  33.5 0.7 %copy.6 = bf16[1,1,16,8,1536]{4,3,2,1,0:T(8,128)(2,1)} copy(bf16[1,1,16,8,1536]{4,3,2,1,0:T(8,128)(2,1)S(1)} %bitcast.5) | data formatting | bytes 786432

commit v5 on v4

--- a/solution.py
+++ b/solution.py
@@ -18,8 +18,8 @@
 DEPTH = 1536
 R_MAIN, R_TOP, L_MAIN, L_TOP = (0, 48, 0, 1), (48, 16, -1, 1), (64, 48, 0, 0), (112, 16, -1, 0)
 PIECES = (L_TOP, L_MAIN, R_TOP, R_MAIN)
-COPIES = 19
-CHUNKS = ((0, 16, 0, 1), (16, 16, 0, 1), (32, 16, 0, 1), R_TOP)
+COPIES = 17
+CHUNKS = ((0, 32, 0, 1), (32, 16, 0, 1), R_TOP)
 
 
 def token_of(place):
@@ -109,7 +109,7 @@
 
     right_in = [
         send(sending, tile.at[1], rows_of(chunk), device(chunk[2], chunk[3], 2))
-        for chunk in (CHUNKS[3], CHUNKS[0], CHUNKS[1], CHUNKS[2])
+        for chunk in (CHUNKS[-1], *CHUNKS[:-1])
     ]
     right_in = [*right_in[1:], right_in[0]]
     sending[left] = jnp.dot(arrange[64:], mine, preferred_element_type=jnp.float32).astype(jnp.bfloat16)

time: 34.4 us -> 35.6 us (1.035)
  Pallas kernels: 33.5 us -> 34.7 us
    pallas_call x1, Pallas kernels: 33.5 us -> 34.7 us  [shards(): pl.pallas_call(kernel, out_shape=pltpu.VMEM((TOKENS, DEPTH), jnp.bfloat16...]
where the time goes in v5:
time: 35.6 us; the launch traced here: 35.4 us
  Pallas kernels  34.7 us (97%)
  local copies, waits for them, and re-layouts  0.75 us (2%)
    pallas_call x1, Pallas kernels, shards(): pl.pallas_call(kernel, out_shape=pltpu.VMEM((TOKENS, DEPTH), jnp.bfloat16...  34.7 us
    unnamed x1, local copies, waits for them, and re-layouts  0.75 us

profile of v5, /device:TPU:2, one launch (start us, length us, event | category | flops | bytes accessed | tf_op | source)
XLA Modules:
  0.0 35.4 jit_solution(10208272561776950708)
XLA Ops:
  0.0 34.7 %shard_map.46 = bf16[128,1536]{1,0:T(8,128)(2,1)S(1)} custom-call(bf16[16,8,1536]{2,1,0:T(8,128)(2,1)} %bitcast.7, bf16[3,1536,384]{2,1,0:T(8,128)(2,1)} %bitcast.6, f32[1,128]{1,0:T(1,128)} %bitcast.8, f32[1,128]{1,0:T(1,128)} %bitcast.9), custom_call_target="tpu_custom_call" | custom-call | tf_op jit(solution)/shard_map/pallas_call | solution.py:194
  34.7 0.7 %copy.6 = bf16[1,1,16,8,1536]{4,3,2,1,0:T(8,128)(2,1)} copy(bf16[1,1,16,8,1536]{4,3,2,1,0:T(8,128)(2,1)S(1)} %bitcast.5) | data formatting | bytes 786432
